TPU v7x, 128 devices: a whole 4x4x4 slice. The times are simulated.
128 devices in a mesh: dp: 4 (over z), seq: 4 (over y), expert: 8 (over x, core).
Axes of the slice: x: 4, y: 4, z: 4, core: 2. Of those that a mesh axis runs over, the one named last changes fastest.
Arguments:
- tokens: bfloat16 [8, 2048, 1024], P('expert', ('dp', 'seq')), may hold values from -6 to 6
- cotangent: bfloat16 [8, 2048, 1024], P('expert', ('dp', 'seq')), may hold values from -6 to 6
- doc_lengths: int32 [8, 4], P('expert'), may hold values from 1 to 2044, as said below
- routes: int32 [8, 2048, 8], P('expert', ('dp', 'seq')), may hold values from 0 to 31, all different within a row
- route_rank: int32 [8, 2048], P('expert', ('dp', 'seq')), may hold values from 0 to 127, as said below
- w_qkv: bfloat16 [1024, 2048], P(('dp', 'seq')), may hold values from -0.1875 to 0.1875
- w_o: bfloat16 [1024, 1024], P(('dp', 'seq')), may hold values from -1.5 to 1.5
- norm_gains: bfloat16 [3, 1024], P(None, ('dp', 'seq')), may hold values from 0.5 to 1.5
- key_gain: bfloat16 [512], P(('dp', 'seq')), may hold values from 0.5 to 1.5
- w_router: bfloat16 [1024, 32], P(('dp', 'seq')), may hold values from -0.09375 to 0.09375
- w_in: bfloat16 [32, 1024, 2, 512], P('expert', ('dp', 'seq')), may hold values from -0.1875 to 0.1875
- w_out: bfloat16 [32, 512, 1024], P('expert', ('dp', 'seq')), may hold values from -1 to 1
Outputs:
- output: bfloat16 [8, 2048, 1024], P('expert', ('dp', 'seq'))
- input_grad: float32 [8, 2048, 1024], P('expert', ('dp', 'seq'))
- grad_qkv: float32 [1024, 2048], P(('dp', 'seq'))
- grad_o: float32 [1024, 1024], P(('dp', 'seq'))
- grad_norm_gains: float32 [3, 1024], P(None, ('dp', 'seq'))
- grad_key_gain: float32 [512], P(('dp', 'seq'))
- grad_router: float32 [1024, 32], P(('dp', 'seq'))
- grad_in: float32 [32, 1024, 2, 512], P('expert', ('dp', 'seq'))
- grad_out: float32 [32, 512, 1024], P('expert', ('dp', 'seq'))
Inputs may be any that keep to these rules, and one draw needn't show every extreme that they name: `routes`: each row names 8 different experts. `doc_lengths`: the 4 documents of a row lie end to end from the sequence's first position; their sum is below 2048, and the positions after it are padding. `route_rank`: within each aligned block of 128 positions of a sequence every number from 0 to 127 stands once.
All inputs are finite; a program needn't handle non-finite values.
Results may differ from a plain program's by a relative error of at most 0.025.
Values may be sent and summed in bfloat16 or wider, within the bound.
No kernel may reach another device: no remote copies, remote signals or barrier semaphores. Data moves between devices by JAX's collectives and lax.ppermute only.
A program may use at most 192 MiB of HBM per device.

v0:
```python
import jax
import jax.numpy as jnp
from jax import lax
from jax.sharding import PartitionSpec as P

HEADS = 16
KV_HEADS = 8
HEAD_DIM = 64
TOPK = 8
HALF = 512


epsilon = 1e-05
highest = lax.Precision.HIGHEST


def extended(array, sides, width):
    for axis, dim in sides:
        size, length = (lax.axis_size(axis), array.shape[dim])
        up = [(i, (i + 1) % size) for i in range(size - 1)]
        down = [(j, i) for i, j in up]
        last = lax.slice_in_dim(array, length - width, length, axis=dim)
        leading = lax.slice_in_dim(array, 0, width, axis=dim)
        before = lax.ppermute(last, axis, up)
        after = lax.ppermute(leading, axis, down)
        array = jnp.concatenate([before, array, after], axis=dim)
    return array


def norm_rows(matrix, gain_row):
    inverse = lax.rsqrt(jnp.mean(matrix * matrix, axis=-1, keepdims=True) + epsilon)
    unit_rows = matrix * inverse
    return (unit_rows * gain_row, unit_rows, inverse)


def norm_back(upstream, unit_rows, inverse, gain_row):
    gain_grad = jnp.sum(upstream * unit_rows, axis=0)
    scaled = upstream * gain_row
    inner_mean = jnp.mean(scaled * unit_rows, axis=-1, keepdims=True)
    return (inverse * (scaled - unit_rows * inner_mean), gain_grad)


def rotate(heads_rows, positions, direction):
    half_dim = heads_rows.shape[-1] // 2
    frequency = 10000.0 ** (-jnp.arange(half_dim, dtype=jnp.float32) / half_dim)
    angles = positions.astype(jnp.float32)[:, None] * frequency[None, :]
    cosine = jnp.cos(angles)[:, None, :]
    sine = direction * jnp.sin(angles)[:, None, :]
    front = heads_rows[..., :half_dim]
    behind = heads_rows[..., half_dim:]
    return jnp.concatenate(
        [front * cosine - behind * sine, behind * cosine + front * sine], axis=-1
    )


def documents(lengths, places):
    ends = jnp.cumsum(lengths)
    doc_ids = jnp.sum((places[:, None] >= ends[None, :]).astype(jnp.int32), axis=1)
    starts = jnp.concatenate([jnp.zeros((1,), jnp.int32), ends])
    marks = jnp.arange(starts.shape[0], dtype=jnp.int32)
    begins = jnp.sum(jnp.where(doc_ids[:, None] == marks[None, :], starts[None, :], 0), axis=1)
    return (doc_ids, places - begins)


def contract_rows(left, right):
    return lax.dot_general(
        left, right, (((0,), (0,)), ((), ())), preferred_element_type=jnp.float32
    )


def contract_cols(left, right):
    return lax.dot_general(
        left, right, (((1,), (1,)), ((), ())), preferred_element_type=jnp.float32
    )


def exact_rows(left, right):
    return lax.dot_general(
        left, right, (((0,), (0,)), ((), ())), precision=highest, preferred_element_type=jnp.float32
    )


def exact_cols(left, right):
    return lax.dot_general(
        left, right, (((1,), (1,)), ((), ())), precision=highest, preferred_element_type=jnp.float32
    )


def over_expert(qkv_grad, out_grad, gain_grad, key_grad, router_grad):
    return (
        lax.psum(qkv_grad.astype(jnp.bfloat16), "expert").astype(jnp.float32),
        lax.psum(out_grad.astype(jnp.bfloat16), "expert").astype(jnp.float32),
        lax.psum(gain_grad.astype(jnp.bfloat16), "expert").astype(jnp.float32),
        lax.psum(key_grad.astype(jnp.bfloat16), "expert").astype(jnp.float32),
        lax.psum(router_grad.astype(jnp.bfloat16), "expert").astype(jnp.float32),
    )


def over_group(qkv_grad, out_grad, gain_grad, key_grad, router_grad, in_grad, down_grad):
    return (
        lax.psum_scatter(
            qkv_grad.astype(jnp.bfloat16), ("dp", "seq"), scatter_dimension=0, tiled=True
        ).astype(jnp.float32),
        lax.psum_scatter(
            out_grad.astype(jnp.bfloat16), ("dp", "seq"), scatter_dimension=0, tiled=True
        ).astype(jnp.float32),
        lax.psum_scatter(
            gain_grad.astype(jnp.bfloat16), ("dp", "seq"), scatter_dimension=1, tiled=True
        ).astype(jnp.float32),
        lax.psum_scatter(
            key_grad.astype(jnp.bfloat16), ("dp", "seq"), scatter_dimension=0, tiled=True
        ).astype(jnp.float32),
        lax.psum_scatter(
            router_grad.astype(jnp.bfloat16), ("dp", "seq"), scatter_dimension=0, tiled=True
        ).astype(jnp.float32),
        lax.psum_scatter(
            in_grad.astype(jnp.bfloat16), ("dp", "seq"), scatter_dimension=1, tiled=True
        ).astype(jnp.float32),
        lax.psum_scatter(
            down_grad.astype(jnp.bfloat16), ("dp", "seq"), scatter_dimension=1, tiled=True
        ).astype(jnp.float32),
    )


def shards(
    tokens,
    cotangent,
    doc_lengths,
    routes,
    route_rank,
    w_qkv,
    w_o,
    norm_gains,
    key_gain,
    w_router,
    w_in,
    w_out,
):
    seq_ways = lax.axis_size("seq")
    expert_ways = lax.axis_size("expert")
    group_size = lax.axis_size(("dp", "seq"))
    qkv_full, out_full, gain_rows, key_gain_full, router_full, in_full, down_full = (
        lax.all_gather(w_qkv, ("dp", "seq"), axis=0, tiled=True),
        lax.all_gather(w_o, ("dp", "seq"), axis=0, tiled=True),
        lax.all_gather(norm_gains, ("dp", "seq"), axis=1, tiled=True),
        lax.all_gather(key_gain, ("dp", "seq"), axis=0, tiled=True),
        lax.all_gather(w_router, ("dp", "seq"), axis=0, tiled=True),
        lax.all_gather(w_in, ("dp", "seq"), axis=1, tiled=True),
        lax.all_gather(w_out, ("dp", "seq"), axis=1, tiled=True),
    )
    token_rows = tokens.shape[1]
    width = qkv_full.shape[0]
    kv_width = key_gain_full.shape[0]
    expert_total = router_full.shape[1]
    local_experts = in_full.shape[0]
    hidden_width = in_full.shape[3]
    capacity = token_rows * TOPK * 5 // (4 * expert_total)
    seq_length = token_rows * group_size
    head_share = width // seq_ways
    kv_share = kv_width // seq_ways
    kv_local = kv_share // HEAD_DIM
    groups_per = HEADS // KV_HEADS
    lengths = doc_lengths[0]
    chosen_ids = routes[0]
    ranking = route_rank[0]
    residual = tokens[0].astype(jnp.float32)
    places = lax.axis_index(("dp", "seq")) * token_rows + jnp.arange(token_rows, dtype=jnp.int32)
    _, positions = documents(lengths, places)
    first_norm, first_unit, first_inverse = norm_rows(residual, gain_rows[0])
    first_low = first_norm.astype(jnp.bfloat16)
    projected = jnp.dot(first_low, qkv_full, preferred_element_type=jnp.float32)
    query_norm, query_unit, query_inverse = norm_rows(projected[:, :width], gain_rows[2])
    key_norm, key_unit, key_inverse = norm_rows(
        projected[:, width : width + kv_width], key_gain_full
    )
    queries = rotate(query_norm.reshape(token_rows, HEADS, HEAD_DIM), positions, 1.0).astype(
        jnp.bfloat16
    )
    keys_rot = rotate(key_norm.reshape(token_rows, KV_HEADS, HEAD_DIM), positions, 1.0).astype(
        jnp.bfloat16
    )
    values_low = projected[:, width + kv_width :].astype(jnp.bfloat16)
    query_send = queries.reshape(token_rows, seq_ways, head_share)
    pair_send = jnp.concatenate(
        [
            keys_rot.reshape(token_rows, seq_ways, kv_share),
            values_low.reshape(token_rows, seq_ways, kv_share),
        ],
        axis=2,
    )
    query_heads, pair_heads = (
        lax.all_to_all(query_send, "seq", split_axis=1, concat_axis=0, tiled=True),
        lax.all_to_all(pair_send, "seq", split_axis=1, concat_axis=0, tiled=True),
    )
    span_rows = query_heads.shape[0]
    pair_heads = pair_heads.reshape(span_rows, 2 * kv_share)
    pair_ext = extended(pair_heads, (("dp", 0),), HALF)
    ext_rows = span_rows + 2 * HALF
    ext_places = lax.axis_index("dp") * span_rows - HALF + jnp.arange(ext_rows, dtype=jnp.int32)
    ext_docs, _ = documents(lengths, ext_places)
    ext_docs = jnp.where((ext_places >= 0) & (ext_places < seq_length), ext_docs, -1)
    own_docs = ext_docs[HALF : HALF + span_rows]
    keys_ext = pair_ext[:, :kv_share].reshape(ext_rows, kv_local, HEAD_DIM)
    values_ext = pair_ext[:, kv_share:].reshape(ext_rows, kv_local, HEAD_DIM)
    query_grouped = query_heads.reshape(span_rows, kv_local, groups_per, HEAD_DIM)
    block_rows = min(512, span_rows)
    block_total = span_rows // block_rows
    window_rows = block_rows + 2 * HALF
    score_scale = HEAD_DIM ** (-0.5)
    offsets = (
        jnp.arange(window_rows, dtype=jnp.int32)[None, :]
        - HALF
        - jnp.arange(block_rows, dtype=jnp.int32)[:, None]
    )
    in_window = (offsets >= -HALF) & (offsets < HALF)

    def block_scores():
        allowed = in_window & (own_docs[:, None] == ext_docs[None, :])
        scores = (
            jnp.einsum(
                "qkgd,mkd->kgqm", query_grouped, keys_ext, preferred_element_type=jnp.float32
            )
            * score_scale
        )
        return (jnp.where(allowed[None, None], scores, -1e30), query_grouped, keys_ext, values_ext)

    def attend_block(block_index):
        scores, _, _, value_block = block_scores()
        largest = jnp.max(scores, axis=-1, keepdims=True)
        weights = jnp.exp(scores - largest)
        totals = jnp.sum(weights, axis=-1, keepdims=True)
        probs = (weights / totals).astype(jnp.bfloat16)
        mixed = jnp.einsum("kgqm,mkd->qkgd", probs, value_block, preferred_element_type=jnp.float32)
        return (
            mixed.reshape(block_rows, head_share).astype(jnp.bfloat16),
            (largest + jnp.log(totals))[..., 0],
        )

    attended, log_totals = lax.map(attend_block, jnp.arange(block_total, dtype=jnp.int32))
    back_send = attended.reshape(seq_ways, token_rows, head_share)
    attn_rows = lax.all_to_all(back_send, "seq", split_axis=0, concat_axis=2, tiled=True).reshape(
        token_rows, width
    )
    middle = residual + jnp.dot(attn_rows, out_full, preferred_element_type=jnp.float32)
    second_norm, second_unit, second_inverse = norm_rows(middle, gain_rows[1])
    second_low = second_norm.astype(jnp.bfloat16)
    logits = jnp.dot(second_low, router_full, preferred_element_type=jnp.float32)
    picked = chosen_ids[:, :, None] == jnp.arange(expert_total, dtype=jnp.int32)[None, None, :]
    chosen = jnp.sum(jnp.where(picked, logits[:, None, :], 0.0), axis=2)
    gates = jax.nn.softmax(chosen, axis=1)
    used = jnp.sum(picked.astype(jnp.bfloat16), axis=1)
    earlier = (ranking[None, :] < ranking[:, None]).astype(jnp.bfloat16)
    before = jnp.dot(earlier, used, preferred_element_type=jnp.float32)
    ahead_count = jnp.sum(jnp.where(picked, before[:, None, :], 0.0), axis=2).astype(jnp.int32)
    kept = ahead_count < capacity
    kept_float = kept.astype(jnp.float32)
    target = jnp.where(kept, chosen_ids * capacity + ahead_count, expert_total * capacity).reshape(
        -1
    )
    owners = jnp.repeat(jnp.arange(token_rows, dtype=jnp.int32), TOPK)
    slot_token = jnp.zeros((expert_total * capacity + 1,), jnp.int32).at[target].set(owners)[:-1]
    slot_fill = jnp.zeros((expert_total * capacity + 1,), jnp.float32).at[target].set(1.0)[:-1]
    slot_gate = (
        jnp.zeros((expert_total * capacity + 1,), jnp.float32)
        .at[target]
        .set(gates.reshape(-1))[:-1]
    )
    dispatch_rows = (second_low[slot_token] * slot_fill[:, None].astype(jnp.bfloat16)).reshape(
        expert_ways, local_experts, capacity, width
    )
    arrived = lax.all_to_all(dispatch_rows, "expert", split_axis=0, concat_axis=2, tiled=True)[0]
    in_matrix = in_full.reshape(local_experts, width, 2 * hidden_width)
    both = jnp.einsum("erd,edf->erf", arrived, in_matrix, preferred_element_type=jnp.float32)
    gate_part = both[..., :hidden_width]
    up_part = both[..., hidden_width:]
    hidden = (jax.nn.silu(gate_part) * up_part).astype(jnp.bfloat16)
    produced = jnp.einsum(
        "erf,efd->erd", hidden, down_full, preferred_element_type=jnp.float32
    ).astype(jnp.bfloat16)
    returned = lax.all_to_all(
        produced[None], "expert", split_axis=2, concat_axis=0, tiled=True
    ).reshape(expert_total * capacity, width)
    where_row = chosen_ids * capacity + jnp.minimum(ahead_count, capacity - 1)
    taken = returned[where_row]
    weight = gates * kept_float
    final = middle + jnp.sum(weight[:, :, None] * taken, axis=1)
    output = final.astype(jnp.bfloat16)
    upstream = cotangent[0].astype(jnp.float32)
    gate_grad = jnp.sum(upstream[:, None, :] * taken, axis=2) * kept_float
    chosen_grad = gates * (gate_grad - jnp.sum(gates * gate_grad, axis=1, keepdims=True))
    logit_grad = jnp.sum(jnp.where(picked, chosen_grad[:, :, None], 0.0), axis=1)
    router_grad = exact_rows(second_low.astype(jnp.float32), logit_grad)
    second_grad = exact_cols(logit_grad, router_full.astype(jnp.float32))
    slot_grad = (upstream[slot_token] * (slot_gate * slot_fill)[:, None]).astype(jnp.bfloat16)
    slot_grad = slot_grad.reshape(expert_ways, local_experts, capacity, width)
    arrived_grad = lax.all_to_all(slot_grad, "expert", split_axis=0, concat_axis=2, tiled=True)[0]
    hidden_grad = jnp.einsum(
        "erd,efd->erf", arrived_grad, down_full, preferred_element_type=jnp.float32
    )
    down_grad = jnp.einsum("erf,erd->efd", hidden, arrived_grad, preferred_element_type=jnp.float32)
    sigmoid_gate = jax.nn.sigmoid(gate_part)
    gate_deriv = hidden_grad * up_part * sigmoid_gate * (1.0 + gate_part * (1.0 - sigmoid_gate))
    up_deriv = hidden_grad * gate_part * sigmoid_gate
    both_grad = jnp.concatenate([gate_deriv, up_deriv], axis=-1).astype(jnp.bfloat16)
    in_grad = jnp.einsum(
        "erd,erf->edf", arrived, both_grad, preferred_element_type=jnp.float32
    ).reshape(local_experts, width, 2, hidden_width)
    arrived_in_grad = jnp.einsum(
        "erf,edf->erd", both_grad, in_matrix, preferred_element_type=jnp.float32
    ).astype(jnp.bfloat16)
    back_rows = lax.all_to_all(
        arrived_in_grad[None], "expert", split_axis=2, concat_axis=0, tiled=True
    ).reshape(expert_total * capacity, width)
    second_grad = second_grad + jnp.sum(back_rows[where_row] * kept_float[:, :, None], axis=1)
    middle_norm_grad, second_gain_grad = norm_back(
        second_grad, second_unit, second_inverse, gain_rows[1]
    )
    middle_grad = upstream + middle_norm_grad
    branch_grad = middle_grad.astype(jnp.bfloat16)
    out_grad = contract_rows(attn_rows, branch_grad)
    attn_grad = contract_cols(branch_grad, out_full).astype(jnp.bfloat16)
    grad_send = attn_grad.reshape(token_rows, seq_ways, head_share)
    heads_grad = lax.all_to_all(grad_send, "seq", split_axis=1, concat_axis=0, tiled=True).reshape(
        span_rows, kv_local, groups_per, HEAD_DIM
    )

    def attend_back(accums, block_index):
        key_accum, value_accum = accums
        scores, query_block, key_block, value_block = block_scores()
        probs = jnp.exp(scores - log_totals[block_index][..., None])
        prob_grad = jnp.einsum(
            "qkgd,mkd->kgqm", heads_grad, value_block, preferred_element_type=jnp.float32
        )
        centre = jnp.sum(probs * prob_grad, axis=-1, keepdims=True)
        score_grad = (probs * (prob_grad - centre)).astype(jnp.bfloat16)
        query_grad = (
            jnp.einsum("kgqm,mkd->qkgd", score_grad, key_block, preferred_element_type=jnp.float32)
            * score_scale
        )
        key_piece = (
            jnp.einsum(
                "kgqm,qkgd->mkd", score_grad, query_block, preferred_element_type=jnp.float32
            )
            * score_scale
        )
        value_piece = jnp.einsum(
            "kgqm,qkgd->mkd",
            probs.astype(jnp.bfloat16),
            heads_grad,
            preferred_element_type=jnp.float32,
        )
        key_accum = key_accum + key_piece
        value_accum = value_accum + value_piece
        return (
            (key_accum, value_accum),
            query_grad.reshape(block_rows, head_share).astype(jnp.bfloat16),
        )

    empty_ext = jnp.zeros((ext_rows, kv_local, HEAD_DIM), jnp.float32)
    (key_ext_grad, value_ext_grad), query_heads_grad = lax.scan(
        attend_back, (empty_ext, empty_ext), jnp.arange(block_total, dtype=jnp.int32)
    )
    pair_ext_grad = jnp.concatenate(
        [key_ext_grad.reshape(ext_rows, kv_share), value_ext_grad.reshape(ext_rows, kv_share)],
        axis=1,
    )
    rim_send = jnp.concatenate([pair_ext_grad[:HALF], pair_ext_grad[HALF + span_rows :]], axis=0)
    rim_back = extended(rim_send.astype(jnp.bfloat16), (("dp", 0),), HALF).astype(rim_send.dtype)
    pair_grad = pair_ext_grad[HALF : HALF + span_rows]
    pair_grad = pair_grad.at[:HALF].add(rim_back[:HALF])
    pair_grad = pair_grad.at[span_rows - HALF :].add(rim_back[3 * HALF :])
    query_back_send = query_heads_grad.reshape(seq_ways, token_rows, head_share)
    pair_back_send = pair_grad.astype(jnp.bfloat16).reshape(seq_ways, token_rows, 2 * kv_share)
    query_rows_grad, pair_rows_grad = (
        lax.all_to_all(query_back_send, "seq", split_axis=0, concat_axis=2, tiled=True),
        lax.all_to_all(pair_back_send, "seq", split_axis=0, concat_axis=2, tiled=True),
    )
    query_rows_grad = query_rows_grad.reshape(token_rows, width).astype(jnp.float32)
    pair_rows_grad = pair_rows_grad.reshape(token_rows, seq_ways, 2, kv_share)
    key_rows_grad = pair_rows_grad[:, :, 0, :].reshape(token_rows, kv_width).astype(jnp.float32)
    value_rows_grad = pair_rows_grad[:, :, 1, :].reshape(token_rows, kv_width)
    query_norm_grad = rotate(
        query_rows_grad.reshape(token_rows, HEADS, HEAD_DIM), positions, -1.0
    ).reshape(token_rows, width)
    key_norm_grad = rotate(
        key_rows_grad.reshape(token_rows, KV_HEADS, HEAD_DIM), positions, -1.0
    ).reshape(token_rows, kv_width)
    query_raw_grad, query_gain_grad = norm_back(
        query_norm_grad, query_unit, query_inverse, gain_rows[2]
    )
    key_raw_grad, key_gain_grad = norm_back(key_norm_grad, key_unit, key_inverse, key_gain_full)
    proj_grad = jnp.concatenate(
        [query_raw_grad.astype(jnp.bfloat16), key_raw_grad.astype(jnp.bfloat16), value_rows_grad],
        axis=1,
    )
    qkv_grad = contract_rows(first_low, proj_grad)
    first_grad = contract_cols(proj_grad, qkv_full)
    input_norm_grad, first_gain_grad = norm_back(
        first_grad, first_unit, first_inverse, gain_rows[0]
    )
    input_grad = middle_grad + input_norm_grad
    gain_grads = jnp.stack([first_gain_grad, second_gain_grad, query_gain_grad])
    qkv_sum, out_sum, gain_sum, key_sum, router_sum = over_expert(
        qkv_grad, out_grad, gain_grads, key_gain_grad, router_grad
    )
    qkv_own, out_own, gain_own, key_own, router_own, in_own, down_own = over_group(
        qkv_sum, out_sum, gain_sum, key_sum, router_sum, in_grad, down_grad
    )
    return (
        output[None],
        input_grad[None],
        qkv_own,
        out_own,
        gain_own,
        key_own,
        router_own,
        in_own,
        down_own,
    )


def solution(mesh):
    return jax.shard_map(
        shards,
        mesh=mesh,
        in_specs=(
            P("expert", ("dp", "seq"), None),
            P("expert", ("dp", "seq"), None),
            P("expert", None),
            P("expert", ("dp", "seq"), None),
            P("expert", ("dp", "seq")),
            P(("dp", "seq"), None),
            P(("dp", "seq"), None),
            P(None, ("dp", "seq")),
            P(("dp", "seq")),
            P(("dp", "seq"), None),
            P("expert", ("dp", "seq"), None, None),
            P("expert", ("dp", "seq"), None),
        ),
        out_specs=(
            P("expert", ("dp", "seq"), None),
            P("expert", ("dp", "seq"), None),
            P(("dp", "seq"), None),
            P(("dp", "seq"), None),
            P(None, ("dp", "seq")),
            P(("dp", "seq")),
            P(("dp", "seq"), None),
            P("expert", ("dp", "seq"), None, None),
            P("expert", ("dp", "seq"), None),
        ),
        check_vma=False,
    )
```

profile of v0, /device:TPU:0, one launch (start us, length us, event | category | flops | bytes accessed | tf_op | source)
XLA Modules:
  0.0 1000.4 jit_solution(5606200196533238092)
XLA Ops:
  10.0 24.9 %all-gather = bf16[16,64,3]{1,2,0:T(4,128)(2,1)S(1)} all-gather(bf16[1,64,3]{1,2,0:T(4,128)(2,1)} %bitcast.261), channel_id=1, replica_groups=mesh['dp'=4,'seq'=4,'expert'=8] {'dp','seq'}, dimensions={0}, use_global_device_ids=true | all-gather | bytes 6528 | tf_op jit(solution)/shard_map/all_gather | solution.py:145
  38.9 38.5 %all-reduce = bf16[512]{0:T(512)(128)(2,1)S(1)} all-reduce(bf16[512]{0:T(512)(128)(2,1)S(1)} %dynamic-update-slice.4), channel_id=1, replica_groups=mesh['dp'=4,'seq'=4,'expert'=8] {'dp','seq'}, use_global_device_ids=true, to_apply=%add | all-reduce | flops 512 | bytes 2048
  89.8 5.5 all-to-all-done
  104.7 24.5 %all-gather.1 = bf16[16,64,32]{1,2,0:T(8,128)(2,1)S(1)} all-gather(bf16[1,64,32]{1,2,0:T(8,128)(2,1)S(1)} %bitcast.257), channel_id=1, replica_groups=mesh['dp'=4,'seq'=4,'expert'=8] {'dp','seq'}, dimensions={0}, use_global_device_ids=true | all-gather | bytes 69632 | tf_op jit(solution)/shard_map/all_gather | solution.py:147
  144.8 6.4 all-to-all-done.2
  174.9 5.3 gather_fusion.2
  193.2 13.5 %all-to-all-done.3 = bf16[8,4,40,1024]{3,2,1,0:T(8,128)(2,1)S(1)} async-done(((bf16[8,4,40,1024]{3,2,1,0:T(8,128)(2,1)}), bf16[8,4,40,1024]{3,2,1,0:T(8,128)(2,1)S(1)}, u32[]{:S(2)}, u32[]{:S(2)}) %all-to-all-start.3) | async-done | bytes 2621472 | tf_op jit(solution)/shard_map/all_to_all | solution.py:271
  213.4 31.0 %all-to-all-done.5 = bf16[8,4,40,1024]{3,2,1,0:T(8,128)(2,1)} async-done(((bf16[8,4,40,1024]{3,2,1,0:T(8,128)(2,1)}), bf16[8,4,40,1024]{3,2,1,0:T(8,128)(2,1)}, u32[]{:S(2)}, u32[]{:S(2)}) %all-to-all-start.5) | async-done | bytes 2621472 | tf_op jit(solution)/shard_map/all_to_all | solution.py:296
  246.5 14.7 %reshape.641 = bf16[4,1024,1024]{2,1,0:T(8,128)(2,1)} reshape(bf16[4,1024,2,512]{3,2,1,0:T(2,128)(2,1)} %all-gather.11.cloned.1.call-done) | data formatting | bytes 16777216 | tf_op jit(solution)/shard_map/reshape | solution.py:272
  261.1 9.3 fusion.73
  270.5 8.2 multiply_convert_fusion.2
  298.3 25.1 %all-to-all-done.6 = bf16[1,4,320,1024]{3,1,0,2:T(4,128)(2,1)S(1)} async-done(((bf16[1,4,320,1024]{3,1,0,2:T(4,128)(2,1)}), bf16[1,4,320,1024]{3,1,0,2:T(4,128)(2,1)S(1)}, u32[]{:S(2)}, u32[]{:S(2)}) %all-to-all-start.6) | async-done | bytes 2621472 | tf_op jit(solution)/shard_map/all_to_all | solution.py:311
  335.2 25.6 %all-to-all-done.4 = bf16[1,4,320,1024]{3,1,0,2:T(4,128)(2,1)} async-done(((bf16[1,4,320,1024]{3,1,0,2:T(4,128)(2,1)}), bf16[1,4,320,1024]{3,1,0,2:T(4,128)(2,1)}, u32[]{:S(2)}, u32[]{:S(2)}) %all-to-all-start.4) | async-done | bytes 2621472 | tf_op jit(solution)/shard_map/all_to_all | solution.py:280
  365.0 5.3 gather_fusion.3
  370.3 8.1 gather_fusion.1
  401.9 6.0 fusion
  407.9 6.8 fusion.2
  417.6 6.7 fusion.5
  435.2 5.3 collective-permute-start.2
  447.1 4.9 all-to-all-start.9
  453.2 5.5 all-to-all-done.9
  470.2 8.5 convolution_convert_fusion
  478.7 14.9 %copy.193 = bf16[4,1024,2,512]{3,0,2,1:T(4,128)(2,1)} copy(bf16[4,1024,2,512]{1,3,2,0:T(8,128)(2,1)} %bitcast.211) | data formatting | bytes 16777216 | tf_op jit(solution)/shard_map/convert_element_type | solution.py:117
  495.4 5.7 convolution_convert_fusion.2
  503.3 43.9 %reduce-scatter.14.cloned.1.call-done = bf16[64,1024]{1,0:T(8,128)(2,1)} async-done(((bf16[1024,1024]{1,0:T(8,128)(2,1)}), bf16[64,1024]{1,0:T(8,128)(2,1)}) %reduce-scatter.14.cloned.1.call-update) | async-done | bytes 131088 | tf_op jit(solution)/shard_map/reduce_scatter | solution.py:104
  547.2 80.4 %reduce-scatter.12.cloned.1.call-done = bf16[64,2048]{1,0:T(8,128)(2,1)} async-done(((bf16[1024,2048]{1,0:T(8,128)(2,1)}), bf16[64,2048]{1,0:T(8,128)(2,1)}) %reduce-scatter.12.cloned.1.call-update) | async-done | bytes 262160 | tf_op jit(solution)/shard_map/reduce_scatter | solution.py:101
  628.7 38.2 %all-reduce.1 = bf16[512]{0:T(512)(128)(2,1)S(1)} all-reduce(bf16[512]{0:T(512)(128)(2,1)S(1)} %copy-done.49), channel_id=5, replica_groups=mesh['dp'=4,'seq'=4,'expert'=8] {'dp','seq'}, use_global_device_ids=true, to_apply=%region_39.40.clone | all-reduce | flops 512 | bytes 2048
  666.9 36.1 %reduce-scatter.16.cloned.1.call-done = bf16[64,3]{1,0:T(8,128)(2,1)} async-done(((bf16[1024,3]{1,0:T(8,128)(2,1)}), bf16[64,3]{1,0:T(8,128)(2,1)}) %reduce-scatter.16.cloned.1.call-update) | async-done | bytes 400
  703.8 13.4 %all-reduce.3 = (bf16[3,64]{1,0:T(4,128)(2,1)S(1)}, bf16[32]{0:T(256)(128)(2,1)S(1)}, bf16[64,32]{0,1:T(8,128)(2,1)S(1)}) all-reduce(bf16[3,64]{1,0:T(4,128)(2,1)S(1)} %copy.206, bf16[32]{0:T(256)(128)(2,1)S(1)} %dynamic-slice.12, bf16[64,32]{0,1:T(8,128)(2,1)S(1)} %copy.208), channel_id=1, replica_groups=mesh['dp'=4,'seq'=4,'expert'=8] {'expert'}, use_global_device_ids=true, to_apply=%region_35.36 | all-reduce | flops 2272 | bytes 9088 | tf_op jit(solution)/shard_map/psum | solution.py:93
  718.9 128.9 %all-reduce.8.cloned.1.call-done = bf16[4,1024,2,512]{3,0,2,1:T(4,128)(2,1)} async-done(((bf16[4,1024,2,512]{3,0,2,1:T(4,128)(2,1)}), bf16[4,1024,2,512]{3,0,2,1:T(4,128)(2,1)}) %all-reduce.8.cloned.1.call-update) | async-done | bytes 8388624
  850.6 77.2 %reduce-scatter.10.cloned.1.call-done = bf16[4,32,1024]{2,1,0:T(8,128)(2,1)} async-done(((bf16[4,512,1024]{2,1,0:T(8,128)(2,1)}), bf16[4,32,1024]{2,1,0:T(8,128)(2,1)}) %reduce-scatter.10.cloned.1.call-update) | async-done | bytes 262160 | tf_op jit(solution)/shard_map/reduce_scatter | solution.py:119
  929.6 60.3 %all-reduce.10.cloned.1.call-done = (bf16[64,2048]{1,0:T(8,128)(2,1)}, bf16[64,1024]{1,0:T(8,128)(2,1)}) async-done(((bf16[64,2048]{1,0:T(8,128)(2,1)}, bf16[64,1024]{1,0:T(8,128)(2,1)}), (bf16[64,2048]{1,0:T(8,128)(2,1)}, bf16[64,1024]{1,0:T(8,128)(2,1)})) %all-reduce.10.cloned.1.call-update) | async-done | bytes 393232 | tf_op jit(solution)/shard_map/psum | solution.py:91
  (315 shorter events, 194.3 us)
Async XLA Ops:
  7.2 73.0 %all-gather.7.cloned.1.call-start = ((), (), s32[]{:S(2)}) async-start(), calls=%async_computation.15 | async-start | bytes 4456448 | tf_op jit(solution)/shard_map/all_gather | solution.py:143
  7.9 136.9 %all-gather.9.cloned.1.call-start = ((), (), s32[]{:S(2)}) async-start(), calls=%async_computation.16 | async-start | bytes 2228224 | tf_op jit(solution)/shard_map/all_gather | solution.py:144
  8.7 237.8 %all-gather.11.cloned.1.call-start = ((), (), s32[]{:S(2)}) async-start(), calls=%async_computation.17 | async-start | bytes 8912896 | tf_op jit(solution)/shard_map/all_gather | solution.py:148
  9.4 261.1 %all-gather.13.cloned.1.call-start = ((), (), s32[]{:S(2)}) async-start(), calls=%async_computation.18 | async-start | bytes 4456448 | tf_op jit(solution)/shard_map/all_gather | solution.py:149
  36.1 47.2 %copy-start.40 = (f32[128]{0:T(128)}, f32[128]{0:T(128)S(1)}, u32[]{:S(2)}) copy-start(f32[128]{0:T(128)S(1)} %add_rsqrt_fusion.3) | copy-start | bytes 1540
  85.2 10.1 %all-to-all-start = ((bf16[128,4,256]{0,2,1:T(8,128)(2,1)}), bf16[128,4,256]{0,2,1:T(8,128)(2,1)S(1)}, u32[]{:S(2)}, u32[]{:S(2)}) async-start(bf16[128,4,256]{0,2,1:T(8,128)(2,1)} %pad_maximum_fusion.10), calls=%async_computation | async-start | bytes 524288 | tf_op jit(solution)/shard_map/all_to_all | solution.py:193
  95.3 34.5 %all-to-all-start.1 = ((bf16[128,4,256]{0,2,1:T(8,128)(2,1)}), bf16[128,4,256]{0,2,1:T(8,128)(2,1)S(1)}, u32[]{:S(2)}, u32[]{:S(2)}) async-start(bf16[128,4,256]{0,2,1:T(8,128)(2,1)} %bitcast.23), calls=%async_computation.1 | async-start | bytes 524288 | tf_op jit(solution)/shard_map/all_to_all | solution.py:192
  98.8 31.3 %collective-permute-start.1 = (bf16[512,256]{1,0:T(8,128)(2,1)S(1)}, bf16[512,256]{1,0:T(8,128)(2,1)S(1)}, u32[]{:S(2)}, u32[]{:S(2)}) collective-permute-start(bf16[512,256]{1,0:T(8,128)(2,1)S(1)} %bitcast.233), channel_id=1, source_target_pairs={{32,0},{64,32},{96,64},{33,1},{65,33},{97,65},{34,2},{66,34},{98,6... | collective-permute-start | bytes 786440 | tf_op jit(solution)/shard_map/ppermute | solution.py:25
  100.1 30.0 %collective-permute-start = (bf16[512,256]{1,0:T(8,128)(2,1)S(1)}, bf16[512,256]{1,0:T(8,128)(2,1)S(1)}, u32[]{:S(2)}, u32[]{:S(2)}) collective-permute-start(bf16[512,256]{1,0:T(8,128)(2,1)S(1)} %bitcast.234), channel_id=1, source_target_pairs={{0,32},{32,64},{64,96},{1,33},{33,65},{65,97},{2,34},{34,66},{66,9... | collective-permute-start | bytes 786440 | tf_op jit(solution)/shard_map/ppermute | solution.py:24
  141.0 10.3 %all-to-all-start.2 = ((bf16[4,128,256]{1,2,0:T(8,128)(2,1)}), bf16[4,128,256]{1,2,0:T(8,128)(2,1)S(1)}, u32[]{:S(2)}, u32[]{:S(2)}) async-start(bf16[4,128,256]{1,2,0:T(8,128)(2,1)} %copy.164), calls=%async_computation.2 | async-start | bytes 524288 | tf_op jit(solution)/shard_map/all_to_all | solution.py:241
  154.6 25.6 %copy-start.30 = (f32[128,8]{0,1:T(8,128)}, f32[128,8]{0,1:T(8,128)S(1)}, u32[]{:S(2)}) copy-start(f32[128,8]{0,1:T(8,128)S(1)} %get-tuple-element.141) | copy-start | bytes 12292
  169.7 37.0 %all-to-all-start.3 = ((bf16[8,4,40,1024]{3,2,1,0:T(8,128)(2,1)}), bf16[8,4,40,1024]{3,2,1,0:T(8,128)(2,1)S(1)}, u32[]{:S(2)}, u32[]{:S(2)}) async-start(bf16[8,4,40,1024]{3,2,1,0:T(8,128)(2,1)} %broadcast_multiply_fusion), calls=%async_computation.3 | async-start | bytes 5242880 | tf_op jit(solution)/shard_map/all_to_all | solution.py:271
  206.7 37.6 %all-to-all-start.5 = ((bf16[8,4,40,1024]{3,2,1,0:T(8,128)(2,1)}), bf16[8,4,40,1024]{3,2,1,0:T(8,128)(2,1)}, u32[]{:S(2)}, u32[]{:S(2)}) async-start(bf16[8,4,40,1024]{3,2,1,0:T(8,128)(2,1)} %multiply_convert_fusion), calls=%async_computation.5 | async-start | bytes 5242880 | tf_op jit(solution)/shard_map/all_to_all | solution.py:296
  287.0 36.4 %all-to-all-start.6 = ((bf16[1,4,320,1024]{3,1,0,2:T(4,128)(2,1)}), bf16[1,4,320,1024]{3,1,0,2:T(4,128)(2,1)S(1)}, u32[]{:S(2)}, u32[]{:S(2)}) async-start(bf16[1,4,320,1024]{3,1,0,2:T(4,128)(2,1)} %copy.176), calls=%async_computation.6 | async-start | bytes 5242880 | tf_op jit(solution)/shard_map/all_to_all | solution.py:311
  298.3 29.7 %copy-start.35 = (f32[2,2,512]{2,1,0:T(2,128)S(1)}, f32[2,2,512]{2,1,0:T(2,128)}, u32[]{:S(2)}) copy-start(f32[2,2,512]{2,1,0:T(2,128)} %copy-done.34) | copy-start | bytes 24580
  298.3 29.7 %copy-start.37 = (f32[2,2,512]{2,1,0:T(2,128)S(1)}, f32[2,2,512]{2,1,0:T(2,128)}, u32[]{:S(2)}) copy-start(f32[2,2,512]{2,1,0:T(2,128)} %copy-done.36) | copy-start | bytes 24580
  298.3 29.7 %copy-start.31 = (f32[128,8]{0,1:T(8,128)S(1)}, f32[128,8]{0,1:T(8,128)}, u32[]{:S(2)}) copy-start(f32[128,8]{0,1:T(8,128)} %copy-done.30) | copy-start | bytes 12292
  323.4 37.4 %all-to-all-start.4 = ((bf16[1,4,320,1024]{3,1,0,2:T(4,128)(2,1)}), bf16[1,4,320,1024]{3,1,0,2:T(4,128)(2,1)}, u32[]{:S(2)}, u32[]{:S(2)}) async-start(bf16[1,4,320,1024]{3,1,0,2:T(4,128)(2,1)} %copy.170), calls=%async_computation.4 | async-start | bytes 5242880 | tf_op jit(solution)/shard_map/all_to_all | solution.py:280
  391.5 10.1 %all-to-all-start.7 = ((bf16[128,4,256]{2,0,1:T(8,128)(2,1)}), bf16[128,4,256]{2,0,1:T(8,128)(2,1)S(1)}, u32[]{:S(2)}, u32[]{:S(2)}) async-start(bf16[128,4,256]{2,0,1:T(8,128)(2,1)} %bitcast.202), calls=%async_computation.7 | async-start | bytes 524288 | tf_op jit(solution)/shard_map/all_to_all | solution.py:323
  394.9 107.6 %reduce-scatter.18.cloned.1.call-start = ((), (), s32[]{:S(2)}) async-start(), calls=%async_computation.23 | async-start | bytes 278528
  395.8 151.4 %reduce-scatter.14.cloned.1.call-start = ((), (), s32[]{:S(2)}) async-start(), calls=%async_computation.21 | async-start | bytes 2228224 | tf_op jit(solution)/shard_map/reduce_scatter | solution.py:104
  429.5 10.9 %all-to-all-start.8 = ((bf16[4,128,256]{1,2,0:T(8,128)(2,1)}), bf16[4,128,256]{1,2,0:T(8,128)(2,1)S(1)}, u32[]{:S(2)}, u32[]{:S(2)}) async-start(bf16[4,128,256]{1,2,0:T(8,128)(2,1)} %copy.182), calls=%async_computation.8 | async-start | bytes 524288 | tf_op jit(solution)/shard_map/all_to_all | solution.py:375
  433.9 11.4 %collective-permute-start.3 = (bf16[512,256]{1,0:T(8,128)(2,1)}, bf16[512,256]{1,0:T(8,128)(2,1)}, u32[]{:S(2)}, u32[]{:S(2)}) collective-permute-start(bf16[512,256]{1,0:T(8,128)(2,1)} %get-tuple-element.155), channel_id=1, source_target_pairs={{32,0},{64,32},{96,64},{33,1},{65,33},{97,65},{34,2},{66,34},{98,6... | collective-permute-start | bytes 786440 | tf_op jit(solution)/shard_map/ppermute | solution.py:25
  435.2 10.1 %collective-permute-start.2 = (bf16[512,256]{1,0:T(8,128)(2,1)}, bf16[512,256]{1,0:T(8,128)(2,1)}, u32[]{:S(2)}, u32[]{:S(2)}) collective-permute-start(bf16[512,256]{1,0:T(8,128)(2,1)} %get-tuple-element.154), channel_id=1, source_target_pairs={{0,32},{32,64},{64,96},{1,33},{33,65},{65,97},{2,34},{34,66},{66,9... | collective-permute-start | bytes 786440 | tf_op jit(solution)/shard_map/ppermute | solution.py:24
  447.1 11.6 %all-to-all-start.9 = ((bf16[4,128,256]{2,1,0:T(8,128)(2,1)}), bf16[4,128,256]{2,1,0:T(8,128)(2,1)S(1)}, u32[]{:S(2)}, u32[]{:S(2)}) async-start(bf16[4,128,256]{2,1,0:T(8,128)(2,1)} %bitcast.236), calls=%async_computation.9 | async-start | bytes 524288 | tf_op jit(solution)/shard_map/all_to_all | solution.py:376
  452.0 175.6 %reduce-scatter.12.cloned.1.call-start = ((), (), s32[]{:S(2)}) async-start(), calls=%async_computation.20 | async-start | bytes 4456448 | tf_op jit(solution)/shard_map/reduce_scatter | solution.py:101
  463.4 239.5 %reduce-scatter.16.cloned.1.call-start = ((), (), s32[]{:S(2)}) async-start(), calls=%async_computation.22 | async-start | bytes 278528
  469.8 377.9 %all-reduce.8.cloned.1.call-start = ((), (), s32[]{:S(2)}) async-start(), calls=%async_computation.24 | async-start | bytes 16777216
  493.6 434.2 %reduce-scatter.10.cloned.1.call-start = ((), (), s32[]{:S(2)}) async-start(), calls=%async_computation.19 | async-start | bytes 4456448 | tf_op jit(solution)/shard_map/reduce_scatter | solution.py:119
  501.1 126.5 %copy-start.27 = (f32[128,1024]{1,0:T(8,128)S(1)}, f32[128,1024]{1,0:T(8,128)}, u32[]{:S(2)}) copy-start(f32[128,1024]{1,0:T(8,128)} %get-tuple-element.185) | copy-start | bytes 1572868
  501.1 127.6 %copy-start.49 = (bf16[512]{0:T(512)(128)(2,1)S(1)}, bf16[512]{0:T(512)(128)(2,1)}, u32[]{:S(2)}) copy-start(bf16[512]{0:T(512)(128)(2,1)} %get-tuple-element.134) | copy-start | bytes 3076
  501.1 488.9 %all-reduce.10.cloned.1.call-start = ((), (), s32[]{:S(2)}) async-start(), calls=%async_computation.25 | async-start | bytes 786432 | tf_op jit(solution)/shard_map/psum | solution.py:91
  (45 other events, 353.7 us)
Sparse Core Ops, SparseCore 0:
  10.2 54.5 all-gather.6
  66.9 46.1 all-gather.8
  115.2 71.2 all-gather.10
  188.5 51.2 all-gather.12
  398.6 71.3 reduce-scatter.17
  473.5 73.7 reduce-scatter.13
  550.6 76.9 reduce-scatter.11
  631.7 71.2 reduce-scatter.15
  706.6 141.1 all-reduce.7
  851.3 76.4 reduce-scatter.9
  930.3 59.6 all-reduce.9
where the time goes:
time: 1010 us; the launch traced here: 1000 us
  waiting for transfers between devices  546 us (54%)
  blocking collectives  139 us (14%)
  local copies, waits for them, and re-layouts  114 us (11%)
  matrix products  83 us (8%)
  starting transfers between devices  52.6 us (5%)
  other arithmetic  47.9 us (5%)
  between operations  17.6 us (2%)
    unnamed x14, waiting for transfers between devices  168 us
    reduce_scatter x1, waiting for transfers between devices, over_group(): lax.psum_scatter(qkv_grad.astype(jnp.bfloat16), ('dp', 'seq'), scatter_di...  80.4 us
    reduce_scatter x1, waiting for transfers between devices, over_group(): lax.psum_scatter(down_grad.astype(jnp.bfloat16), ('dp', 'seq'), scatter_d...  77.2 us
    unnamed x2, blocking collectives  76.7 us
    psum x1, waiting for transfers between devices, over_expert(): lax.psum(qkv_grad.astype(jnp.bfloat16), 'expert').astype(jnp.float32)  60.3 us
    reduce_scatter x1, waiting for transfers between devices, over_group(): lax.psum_scatter(out_grad.astype(jnp.bfloat16), ('dp', 'seq'), scatter_di...  43.9 us
    all_to_all x1, waiting for transfers between devices, shards(): lax.all_to_all(slot_grad, 'expert', split_axis=0, concat_axis=2, tiled=True)  31 us
    all_to_all x1, waiting for transfers between devices, shards(): lax.all_to_all(produced[None], 'expert', split_axis=2, concat_axis=0, til...  25.6 us
  transfers between devices with their start and end apart: 25, of which 14 were waited for; matrix products, arithmetic and copies ran while one was open for 19% of the time, Pallas kernels for 0%

commit v1 on v0

v1 whole, which is shorter than its diff:
```python
import jax
import jax.numpy as jnp
from jax import lax
from jax.sharding import PartitionSpec as P

HEADS = 16
KV_HEADS = 8
HEAD_DIM = 64
TOPK = 8
HALF = 512
CAP = 40

GROUP = ("dp", "seq")
ALL = ("dp", "seq", "expert")
epsilon = 1e-05
highest = lax.Precision.HIGHEST
bf16 = jnp.bfloat16
f32 = jnp.float32


def swap(array, axis):
    return lax.all_to_all(array, axis, split_axis=0, concat_axis=0, tiled=True)


def spread(array, axis, ways):
    return swap(jnp.broadcast_to(array[None], (ways,) + array.shape), axis)


def halo(array):
    size = lax.axis_size("dp")
    up = [(i, i + 1) for i in range(size - 1)]
    down = [(i + 1, i) for i in range(size - 1)]
    return lax.ppermute(array, "dp", up), lax.ppermute(array, "dp", down)


def turn(array, cosine, sine):
    rows, width = array.shape
    heads = array.reshape(rows, width // HEAD_DIM, HEAD_DIM)
    front, behind = heads[..., :32], heads[..., 32:]
    c, s = cosine[:, None, :], sine[:, None, :]
    return jnp.concatenate([front * c - behind * s, behind * c + front * s], axis=-1).reshape(rows, width)


def documents(lengths, places):
    ends = jnp.cumsum(lengths)
    ids = jnp.sum((places[:, None] >= ends[None, :]).astype(jnp.int32), axis=1)
    starts = jnp.concatenate([jnp.zeros((1,), jnp.int32), ends])
    marks = jnp.arange(starts.shape[0], dtype=jnp.int32)
    begins = jnp.sum(jnp.where(ids[:, None] == marks[None, :], starts[None, :], 0), axis=1)
    return ids, places - begins


def dot(a, b, dims, **kw):
    return lax.dot_general(a, b, ((dims[0], dims[1]), ((), ())), preferred_element_type=f32, **kw)


def shards(tokens, cotangent, doc_lengths, routes, route_rank, w_qkv, w_o, norm_gains, key_gain, w_router, w_in, w_out):
    D = 1024
    KVW = 512
    d_index = lax.axis_index("dp")
    s_index = lax.axis_index("seq")
    e_index = lax.axis_index("expert")
    lengths = doc_lengths[0]
    tok_own = tokens[0]
    w_send = jnp.concatenate(
        [
            w_qkv[:, :1024].reshape(64, 4, 256),
            w_qkv[:, 1024:1536].reshape(64, 4, 128),
            w_qkv[:, 1536:].reshape(64, 4, 128),
        ],
        axis=2,
    ).transpose(1, 0, 2)
    extra = jnp.zeros((64, 128), bf16)
    extra = extra.at[:, :32].set(w_router).at[:, 32:35].set(norm_gains.T).at[:32, 35].set(key_gain)
    w_send = jnp.concatenate([w_send, jnp.broadcast_to(extra[None], (4, 64, 128))], axis=2)
    w_send = jnp.broadcast_to(w_send[None], (4, 4, 64, 640)).reshape(16, 64, 640)
    w_got = swap(w_send, GROUP)
    w_cols = w_got[:, :, :512].reshape(1024, 512)
    extras = w_got[:, :, 512:].reshape(1024, 128)
    router = extras[:, :32]
    gain_rows = extras[:, 32:35].T.astype(f32)
    key_full = extras[:, 35].reshape(16, 64)[:, :32].reshape(512).astype(f32)
    span_tokens = spread(tok_own, "seq", 4).reshape(512, D)
    moe_shard = jnp.concatenate([w_in.reshape(4, 64, 1024), w_out], axis=1)
    moe_all = lax.all_gather(moe_shard, GROUP, axis=0, tiled=False)
    out_full = spread(w_o, GROUP, 16).reshape(1024, 1024)
    info = jnp.concatenate([routes[0].T, route_rank], axis=0)
    infos = spread(info, "expert", 8)
    upstream_all = spread(cotangent[0], "expert", 8)

    ext_places = d_index * 512 - HALF + jnp.arange(1536, dtype=jnp.int32)
    ids, positions = documents(lengths, ext_places)
    ext_docs = jnp.where((ext_places >= 0) & (ext_places < 2048), ids, -1)
    own_docs = ext_docs[HALF : HALF + 512]
    frequency = 10000.0 ** (-jnp.arange(32, dtype=f32) / 32)
    angles = positions.astype(f32)[:, None] * frequency[None, :]
    cosine, sine = jnp.cos(angles), jnp.sin(angles)

    span = span_tokens.astype(f32)
    first_inverse = lax.rsqrt(jnp.mean(span * span, axis=-1, keepdims=True) + epsilon)
    first_low = (span * first_inverse * gain_rows[0]).astype(bf16)
    projected = dot(first_low, w_cols, ((1,), (0,)))
    q_raw, k_raw, v_raw = projected[:, :256], projected[:, 256:384], projected[:, 384:]
    kv_low = projected[:, 256:].astype(bf16)
    part = jnp.concatenate(
        [jnp.sum(q_raw * q_raw, axis=1).reshape(4, 128), jnp.sum(k_raw * k_raw, axis=1).reshape(4, 128)], axis=0
    )
    kv_before, kv_after = halo(kv_low)
    parts = spread(part, GROUP, 16).reshape(4, 4, 8, 128)
    sums = jnp.sum(parts, axis=1)
    q_sum = lax.dynamic_index_in_dim(sums, d_index, 0, keepdims=False)[:4].reshape(512)
    k_pad = jnp.pad(sums[:, 4:], ((1, 1), (0, 0), (0, 0)))
    k_sum = lax.dynamic_slice_in_dim(k_pad, d_index, 3, 0).reshape(1536)
    q_inverse = lax.rsqrt(q_sum / 1024 + epsilon)[:, None]
    k_inverse = lax.rsqrt(k_sum / 512 + epsilon)[:, None]
    q_gain = lax.dynamic_slice_in_dim(gain_rows[2], s_index * 256, 256, 0)
    k_gain = lax.dynamic_slice_in_dim(key_full, s_index * 128, 128, 0)
    kv_ext = jnp.concatenate([kv_before, kv_low, kv_after], axis=0)
    q_unit = q_raw * q_inverse
    own_cos, own_sin = cosine[HALF : HALF + 512], sine[HALF : HALF + 512]
    queries = turn(q_unit * q_gain, own_cos, own_sin).astype(bf16)
    keys = turn(kv_ext[:, :128].astype(f32) * k_inverse * k_gain, cosine, sine).astype(bf16)
    values = kv_ext[:, 128:].reshape(1536, 2, 64)
    queries_g = queries.reshape(512, 2, 2, 64)
    keys_g = keys.reshape(1536, 2, 64)
    offsets = jnp.arange(1536, dtype=jnp.int32)[None, :] - HALF - jnp.arange(512, dtype=jnp.int32)[:, None]
    allowed = (offsets >= -HALF) & (offsets < HALF) & (own_docs[:, None] == ext_docs[None, :])

    def get_scores():
        scores = jnp.einsum("qkgd,mkd->kgqm", queries_g, keys_g, preferred_element_type=f32) * 0.125
        return jnp.where(allowed[None, None], scores, -1e30)

    scores = get_scores()
    largest = jnp.max(scores, axis=-1, keepdims=True)
    weights = jnp.exp(scores - largest)
    totals = jnp.sum(weights, axis=-1, keepdims=True)
    probs = (weights / totals).astype(bf16)
    mixed = jnp.einsum("kgqm,mkd->qkgd", probs, values, preferred_element_type=f32)
    attended = mixed.reshape(512, 256).astype(bf16)
    log_totals = largest + jnp.log(totals)
    attn_span = spread(attended, "seq", 4)
    attn_rows = lax.dynamic_slice_in_dim(attn_span, s_index * 128, 128, 1).transpose(1, 0, 2).reshape(128, 1024)
    residual = tok_own.astype(f32)
    middle = residual + dot(attn_rows, out_full, ((1,), (0,)))
    second_inverse = lax.rsqrt(jnp.mean(middle * middle, axis=-1, keepdims=True) + epsilon)
    second_unit = middle * second_inverse
    second_low = (second_unit * gain_rows[1]).astype(bf16)
    normed_all = spread(second_low, "expert", 8)

    def routing(route_t, rank):
        used = jnp.any(route_t[None] == jnp.arange(32, dtype=jnp.int32)[:, None, None], axis=1)
        earlier = (rank[:, None] < rank[None, :]).astype(bf16)
        before = dot(used.astype(bf16), earlier, ((1,), (0,)))
        return used, before.astype(jnp.int32)

    used_all, before_all = jax.vmap(routing)(infos[:, :8], infos[:, 8])
    pos_all = jnp.where(used_all & (before_all < CAP), before_all, -1)
    pos_mine = lax.dynamic_slice_in_dim(pos_all, e_index * 4, 4, 1)
    place = (pos_mine[:, :, None, :] == jnp.arange(CAP, dtype=jnp.int32)[None, None, :, None]).astype(bf16)
    logits_all = jnp.einsum("jtd,de->jte", normed_all, router, preferred_element_type=f32)

    def gates_of(logits, used_t):
        masked = jnp.where(used_t, logits, -1e30)
        top = jnp.max(masked, axis=-1, keepdims=True)
        ex = jnp.where(used_t, jnp.exp(masked - top), 0.0)
        return ex / jnp.sum(ex, axis=-1, keepdims=True)

    gates_all = gates_of(logits_all, used_all.transpose(0, 2, 1))
    gates_mine = lax.dynamic_slice_in_dim(gates_all, e_index * 4, 4, 2)
    slots = jnp.einsum("jlct,jtd->ljcd", place, normed_all, preferred_element_type=f32).astype(bf16).reshape(4, 320, D)
    slot_up = jnp.einsum("jlct,jtd->ljcd", place, upstream_all, preferred_element_type=f32)
    slot_gate = jnp.einsum("jlct,jtl->ljc", place.astype(f32), gates_mine, precision=highest)[..., None]
    slot_grad = (slot_up * slot_gate).astype(bf16).reshape(4, 320, D)
    in_matrix = moe_all[:, :, :64].transpose(1, 0, 2, 3).reshape(4, 1024, 1024)
    out_matrix = moe_all[:, :, 64:].transpose(1, 0, 2, 3).reshape(4, 512, 1024)
    both = jnp.einsum("erd,edf->erf", slots, in_matrix, preferred_element_type=f32)
    gate_part, up_part = both[..., :512], both[..., 512:]
    sig = jax.nn.sigmoid(gate_part)
    hidden = (gate_part * sig * up_part).astype(bf16)
    produced = jnp.einsum("erf,efd->erd", hidden, out_matrix, preferred_element_type=f32).astype(bf16)
    produced_j = produced.reshape(4, 8, CAP, D)
    slot_dgate = jnp.sum(slot_up * produced_j.astype(f32), axis=-1)
    dgate_mine = jnp.einsum("jlct,ljc->jtl", place.astype(f32), slot_dgate, precision=highest)
    weighted = (produced_j.astype(f32) * slot_gate).astype(bf16)
    out_part = jnp.einsum("jlct,ljcd->jtd", place, weighted, preferred_element_type=f32).astype(bf16)
    hidden_grad = jnp.einsum("erd,efd->erf", slot_grad, out_matrix, preferred_element_type=f32)
    gate_deriv = hidden_grad * up_part * sig * (1.0 + gate_part * (1.0 - sig))
    up_deriv = hidden_grad * gate_part * sig
    both_grad = jnp.concatenate([gate_deriv, up_deriv], axis=-1).astype(bf16)
    slot_dx = jnp.einsum("erf,edf->erd", both_grad, in_matrix, preferred_element_type=f32).astype(bf16)
    dn2_part = jnp.einsum(
        "jlct,ljcd->jtd", place, slot_dx.reshape(4, 8, CAP, D), preferred_element_type=f32
    ).astype(bf16)
    dgate_send = lax.dynamic_update_slice(jnp.zeros((8, 128, 128), bf16), dgate_mine.astype(bf16), (0, 0, e_index * 4))
    back = swap(jnp.concatenate([dn2_part, dgate_send], axis=2), "expert")
    in_grad = jnp.einsum("erd,erf->edf", slots, both_grad, preferred_element_type=f32).astype(bf16)
    down_grad = jnp.einsum("erf,erd->efd", hidden, slot_grad, preferred_element_type=f32).astype(bf16)
    moe_grad = jnp.concatenate(
        [in_grad.reshape(4, 16, 64, 1024), down_grad.reshape(4, 16, 32, 1024)], axis=2
    ).transpose(1, 0, 2, 3)
    moe_own = lax.psum_scatter(moe_grad.reshape(16 * 384, 1024), GROUP, scatter_dimension=0, tiled=True)
    moe_own = moe_own.reshape(4, 96, 1024).astype(f32)
    in_own = moe_own[:, :64].reshape(4, 64, 2, 512)
    down_own = moe_own[:, 64:]
    outs = swap(out_part, "expert")
    output = (middle + jnp.sum(outs.astype(f32), axis=0)).astype(bf16)
    back_sum = jnp.sum(back.astype(f32), axis=0)
    dgates = back_sum[:, 1024:1056]
    used_own = lax.dynamic_index_in_dim(used_all, e_index, 0, keepdims=False).T
    logits = dot(second_low, router, ((1,), (0,)))
    gates = gates_of(logits, used_own)
    logit_grad = gates * (dgates - jnp.sum(gates * dgates, axis=-1, keepdims=True))
    router_grad = dot(logit_grad, second_low.astype(f32), ((0,), (0,)), precision=highest)
    dn2 = back_sum[:, :1024] + dot(logit_grad, router.astype(f32), ((1,), (1,)), precision=highest)
    second_gain_grad = jnp.sum(dn2 * second_unit, axis=0)
    scaled = dn2 * gain_rows[1]
    upstream = cotangent[0].astype(f32)
    middle_grad = upstream + second_inverse * (
        scaled - second_unit * jnp.mean(scaled * second_unit, axis=-1, keepdims=True)
    )
    branch = middle_grad.astype(bf16)
    dattn = dot(branch, out_full, ((1,), (1,))).astype(bf16)
    grad_send = jnp.concatenate(
        [dattn.reshape(128, 4, 256).transpose(1, 0, 2), branch.reshape(128, 4, 256).transpose(1, 0, 2)], axis=2
    )
    grad_got = swap(grad_send, "seq").reshape(512, 512)
    heads_grad = grad_got[:, :256].reshape(512, 2, 2, 64)
    branch_cols = grad_got[:, 256:]
    scores = get_scores()
    probs = jnp.exp(scores - log_totals)
    prob_grad = jnp.einsum("qkgd,mkd->kgqm", heads_grad, values, preferred_element_type=f32)
    centre = jnp.sum(probs * prob_grad, axis=-1, keepdims=True)
    score_grad = (probs * (prob_grad - centre)).astype(bf16)
    dq = (jnp.einsum("kgqm,mkd->qkgd", score_grad, keys_g, preferred_element_type=f32) * 0.125).reshape(512, 256)
    dk = (jnp.einsum("kgqm,qkgd->mkd", score_grad, queries_g, preferred_element_type=f32) * 0.125).reshape(1536, 128)
    dv = jnp.einsum("kgqm,qkgd->mkd", probs.astype(bf16), heads_grad, preferred_element_type=f32).reshape(1536, 128)
    dq = dq.astype(bf16).astype(f32)
    dkv = jnp.concatenate([dk, dv], axis=1)
    dkv_low = dkv.astype(bf16)
    up, down = halo_back(dkv_low)
    q_dot = jnp.sum(dq * queries.astype(f32), axis=1).reshape(1, 4, 128)
    k_dot = jnp.sum(dk * keys.astype(f32), axis=1).reshape(3, 4, 128)
    q_place = lax.dynamic_update_slice(jnp.zeros((4, 4, 128), f32), q_dot, (d_index, 0, 0))
    k_place = lax.dynamic_update_slice(jnp.zeros((6, 4, 128), f32), k_dot, (d_index, 0, 0))[1:5]
    dots = jnp.concatenate([q_place, k_place], axis=1)
    dots = swap(jnp.broadcast_to(dots[:, None], (4, 4, 8, 128)).reshape(16, 8, 128), GROUP)
    dots = jnp.sum(dots, axis=0)
    q_mean = dots[:4].reshape(512, 1) / 1024
    k_mean = dots[4:].reshape(512, 1) / 512
    dkv_own = dkv[HALF : HALF + 512] + up.astype(f32) + down.astype(f32)
    wq = turn(dq, own_cos, -own_sin)
    wk = turn(dkv_own[:, :128].astype(bf16).astype(f32), own_cos, -own_sin)
    own_k_inverse = k_inverse[HALF : HALF + 512]
    k_unit = k_raw * own_k_inverse
    q_gain_grad = jnp.sum(wq * q_unit, axis=0)
    k_gain_grad = jnp.sum(wk * k_unit, axis=0)
    dq_raw = q_inverse * (wq * q_gain - q_unit * q_mean)
    dk_raw = own_k_inverse * (wk * k_gain - k_unit * k_mean)
    dqkv = jnp.concatenate([dq_raw, dk_raw, dkv_own[:, 128:]], axis=1).astype(bf16)
    dn1_part = dot(dqkv, w_cols, ((1,), (1,))).astype(bf16)
    dn1 = jnp.sum(swap(dn1_part.reshape(4, 128, 1024), "seq").astype(f32), axis=0)
    own_span = residual
    own_inverse = lax.rsqrt(jnp.mean(own_span * own_span, axis=-1, keepdims=True) + epsilon)
    own_unit = own_span * own_inverse
    scaled1 = dn1 * gain_rows[0]
    input_grad = middle_grad + own_inverse * (
        scaled1 - own_unit * jnp.mean(scaled1 * own_unit, axis=-1, keepdims=True)
    )
    qkv_part = dot(first_low, dqkv, ((0,), (0,)))
    attn_all = attn_span.transpose(1, 0, 2).reshape(512, 1024)
    o_part = dot(attn_all, branch_cols, ((0,), (0,)))
    q_row = lax.dynamic_update_slice(jnp.zeros((1024,), f32), q_gain_grad, (s_index * 256,))
    k_row = lax.dynamic_update_slice(jnp.zeros((512,), f32), k_gain_grad, (s_index * 128,))
    k_row = jnp.pad(k_row.reshape(16, 32), ((0, 0), (0, 32))).reshape(1024)
    small = jnp.concatenate(
        [router_grad, second_gain_grad[None], q_row[None], k_row[None], jnp.zeros((29, 1024), f32)], axis=0
    ).astype(bf16)
    small = small.reshape(8, 8, 16, 64).transpose(2, 0, 1, 3).reshape(128, 8, 64)
    final_send = jnp.concatenate(
        [qkv_part.astype(bf16).reshape(128, 8, 512), o_part.astype(bf16).reshape(128, 8, 256), small], axis=2
    )
    final_got = swap(final_send, ALL).astype(f32)
    by_seq = jnp.sum(final_got.reshape(4, 4, 8, 8, 832), axis=(0, 2))
    small_sum = jnp.sum(by_seq[:, :, 768:], axis=0)
    own = jnp.concatenate(
        [
            by_seq[:, :, :256].transpose(1, 0, 2).reshape(8, 1024),
            by_seq[:, :, 256:384].transpose(1, 0, 2).reshape(8, 512),
            by_seq[:, :, 384:512].transpose(1, 0, 2).reshape(8, 512),
            by_seq[:, :, 512:768].transpose(1, 0, 2).reshape(8, 1024),
            small_sum,
        ],
        axis=1,
    ).astype(bf16)
    rows = spread(own, "expert", 8).astype(f32)
    qkv_own = rows[:, :, :2048].reshape(64, 2048)
    o_own = rows[:, :, 2048:3072].reshape(64, 1024)
    small_own = rows[:, :, 3072:].reshape(64, 64)
    first_gain_own = jnp.sum(qkv_own * w_qkv.astype(f32), axis=1) / norm_gains[0].astype(f32)
    gains_own = jnp.stack([first_gain_own, small_own[32], small_own[33]])
    key_own = small_own[34, :32]
    router_own = small_own[:32].T
    return (output[None], input_grad[None], qkv_own, o_own, gains_own, key_own, router_own, in_own, down_own)


def halo_back(dkv_low):
    size = lax.axis_size("dp")
    up = [(i, i + 1) for i in range(size - 1)]
    down = [(i + 1, i) for i in range(size - 1)]
    return lax.ppermute(dkv_low[1024:], "dp", up), lax.ppermute(dkv_low[:512], "dp", down)


def solution(mesh):
    both = P("expert", GROUP, None)
    rows = P(GROUP, None)
    return jax.shard_map(
        shards,
        mesh=mesh,
        in_specs=(
            both,
            both,
            P("expert", None),
            both,
            P("expert", GROUP),
            rows,
            rows,
            P(None, GROUP),
            P(GROUP),
            rows,
            P("expert", GROUP, None, None),
            P("expert", GROUP, None),
        ),
        out_specs=(
            both,
            both,
            rows,
            rows,
            P(None, GROUP),
            P(GROUP),
            rows,
            P("expert", GROUP, None, None),
            P("expert", GROUP, None),
        ),
        check_vma=False,
    )
```

time: 1010 us -> 538 us (0.53)
  waiting for transfers between devices: 546 us -> 172 us
  blocking collectives: 139 us -> 58.3 us
  local copies, waits for them, and re-layouts: 114 us -> 71.5 us
  starting transfers between devices: 52.6 us -> 72.1 us
    reduce_scatter x3 -> x1, waiting for transfers between devices: 202 us -> 0.01 us  [shards(): lax.psum_scatter(moe_grad.reshape(16 * 384, 1024), GROUP, scatter_dimensi...]
    unnamed x14 -> x2, waiting for transfers between devices: 168 us -> 0.03 us
    unnamed x2 -> x0, blocking collectives: 76.7 us -> none
    psum x1 -> x0, waiting for transfers between devices: 60.3 us -> none  [over_expert(): lax.psum(qkv_grad.astype(jnp.bfloat16), 'expert').astype(jnp.float32)]
    all_to_all x0 -> x2, blocking collectives: none -> 58.3 us  [swap(): return lax.all_to_all(array, axis, split_axis=0, concat_axis=0, tiled=True)]
    all_to_all x10 -> x13, waiting for transfers between devices: 116 us -> 172 us  [swap(): return lax.all_to_all(array, axis, split_axis=0, concat_axis=0, tiled=True)]
    all_gather x2 -> x0, blocking collectives: 49.4 us -> none  [the longest x1 24.9 us: shards(): lax.all_gather(norm_gains, ('dp', 'seq'), axis=1, tiled=True)]
    gather x4 -> x0, local copies, waits for them, and re-layouts: 23 us -> none  [the longest x1 8.11 us: shards(): taken = returned[where_row]]
  transfers between devices with their start and end apart: 25 -> 19, of which waited for: 14 -> 12; matrix products, arithmetic and copies ran while one was open for 19% -> 26% of each run, Pallas kernels for 0% -> 0%
where the time goes in v1:
time: 538 us; the launch traced here: 530 us
  waiting for transfers between devices  172 us (32%)
  matrix products  84.7 us (16%)
  starting transfers between devices  72.1 us (13%)
  local copies, waits for them, and re-layouts  71.5 us (13%)
  blocking collectives  58.3 us (11%)
  other arithmetic  54.6 us (10%)
  between operations  16.4 us (3%)
    all_to_all x13, waiting for transfers between devices, swap(): return lax.all_to_all(array, axis, split_axis=0, concat_axis=0, tiled=True)  172 us
    all_to_all x13, starting transfers between devices, swap(): return lax.all_to_all(array, axis, split_axis=0, concat_axis=0, tiled=True)  59.4 us
    all_to_all x2, blocking collectives, swap(): return lax.all_to_all(array, axis, split_axis=0, concat_axis=0, tiled=True)  58.3 us
    transpose x2, local copies, waits for them, and re-layouts, shards(): in_matrix = moe_all[:, :, :64].transpose(1, 0, 2, 3).reshape(4, 1024, 1024)  16.9 us
    unnamed x200, local copies, waits for them, and re-layouts  15.2 us
    dot_general x10, matrix products, dot(): lax.dot_general(a, b, ((dims[0], dims[1]), ((), ())), preferred_element_t...  12.7 us
    dot_general x1, matrix products, shards(): jnp.einsum('qkgd,mkd->kgqm', heads_grad, values, preferred_element_type=f32)  11.6 us
  transfers between devices with their start and end apart: 19, of which 12 were waited for; matrix products, arithmetic and copies ran while one was open for 26% of the time, Pallas kernels for 0%

profile of v1, /device:TPU:0, one launch (start us, length us, event | category | flops | bytes accessed | tf_op | source)
XLA Modules:
  0.0 529.8 jit_solution(14133906102951143840)
XLA Ops:
  11.8 4.5 all-to-all-start
  25.1 11.4 %all-to-all-done = bf16[4,128,1024]{2,1,0:T(8,128)(2,1)S(1)} async-done(((bf16[4,128,1024]{2,1,0:T(8,128)(2,1)}), bf16[4,128,1024]{2,1,0:T(8,128)(2,1)S(1)}, u32[]{:S(2)}, u32[]{:S(2)}) %all-to-all-start) | async-done | bytes 1048608 | tf_op jit(solution)/shard_map/all_to_all | solution.py:22
  37.9 6.9 %all-to-all-start.1 = ((bf16[16,64,640]{2,1,0:T(8,128)(2,1)}), bf16[16,64,640]{2,1,0:T(8,128)(2,1)S(1)}, u32[]{:S(2)}, u32[]{:S(2)}) async-start(bf16[16,64,640]{2,1,0:T(8,128)(2,1)} %bitcast.360), calls=%async_computation.1 | async-start | bytes 2621440 | tf_op jit(solution)/shard_map/all_to_all | solution.py:22
  47.8 14.6 %all-to-all-done.1 = bf16[16,64,640]{2,1,0:T(8,128)(2,1)S(1)} async-done(((bf16[16,64,640]{2,1,0:T(8,128)(2,1)}), bf16[16,64,640]{2,1,0:T(8,128)(2,1)S(1)}, u32[]{:S(2)}, u32[]{:S(2)}) %all-to-all-start.1) | async-done | bytes 1310752 | tf_op jit(solution)/shard_map/all_to_all | solution.py:22
  65.9 5.3 collective-permute-start
  76.2 8.0 %all-to-all-done.2 = f32[16,8,128]{2,1,0:T(8,128)S(1)} async-done(((f32[16,8,128]{2,1,0:T(8,128)}), f32[16,8,128]{2,1,0:T(8,128)S(1)}, u32[]{:S(2)}, u32[]{:S(2)}) %all-to-all-start.2) | async-done | bytes 65568 | tf_op jit(solution)/shard_map/all_to_all | solution.py:22
  95.7 27.5 %all_to_all.75 = bf16[4,512,256]{1,2,0:T(8,128)(2,1)} all-to-all(bf16[4,512,256]{1,2,0:T(8,128)(2,1)S(1)} %broadcast_in_dim.105), channel_id=1, replica_groups=mesh['dp'=4,'seq'=4,'expert'=8] {'seq'}, dimensions={0} | all-to-all | bytes 2097152 | tf_op jit(solution)/shard_map/all_to_all | solution.py:22
  124.8 4.9 all-to-all-start.4
  130.7 26.4 %all-to-all-done.4 = bf16[16,64,1024]{2,1,0:T(8,128)(2,1)S(1)} async-done(((bf16[16,64,1024]{2,1,0:T(8,128)(2,1)}), bf16[16,64,1024]{2,1,0:T(8,128)(2,1)S(1)}, u32[]{:S(2)}, u32[]{:S(2)}) %all-to-all-start.4) | async-done | bytes 2097184 | tf_op jit(solution)/shard_map/all_to_all | solution.py:22
  167.8 30.8 %all_to_all.76 = bf16[8,128,1024]{2,1,0:T(8,128)(2,1)} all-to-all(bf16[8,128,1024]{2,1,0:T(8,128)(2,1)S(1)} %broadcast_in_dim.109), channel_id=1, replica_groups=mesh['dp'=4,'seq'=4,'expert'=8] {'expert'}, dimensions={0} | all-to-all | bytes 4194304 | tf_op jit(solution)/shard_map/all_to_all | solution.py:22
  212.9 19.0 %all-to-all-done.8 = bf16[8,128,1024]{2,1,0:T(8,128)(2,1)} async-done(((bf16[8,128,1024]{2,1,0:T(8,128)(2,1)}), bf16[8,128,1024]{2,1,0:T(8,128)(2,1)}, u32[]{:S(2)}, u32[]{:S(2)}) %all-to-all-start.8) | async-done | bytes 2097184 | tf_op jit(solution)/shard_map/all_to_all | solution.py:22
  231.9 4.8 fusion.10
  241.1 8.4 %slice_bitcast_fusion = bf16[4,16,64,1024]{3,2,0,1:T(8,128)(2,1)} fusion(bf16[16,4,96,1024]{3,2,1,0:T(8,128)(2,1)} %bitcast.343), kind=kLoop, calls=%fused_computation.13 | loop fusion | bytes 16777216 | tf_op jit(solution)/shard_map/transpose | solution.py:174
  249.6 8.4 %copy.107 = bf16[4,16,64,1024]{3,2,1,0:T(8,128)(2,1)} copy(bf16[4,16,64,1024]{3,2,0,1:T(8,128)(2,1)} %slice_bitcast_fusion) | data formatting | bytes 16777216 | tf_op jit(solution)/shard_map/transpose | solution.py:174
  258.5 4.4 copy-done.8
  262.9 4.8 fusion.118
  274.1 6.8 %convolution_convert_fusion = bf16[4,1024,1024]{2,1,0:T(8,128)(2,1)} fusion(bf16[4,320,1024]{2,1,0:T(8,128)(2,1)S(1)} %bitcast.365, bf16[4,320,512]{2,1,0:T(8,128)(2,1)S(1)} %get-tuple-element.52, bf16[4,320,512]{2,1,0:T(8,128)(2,1)S(1)} %get-tuple-element.51), kind=kOutput, calls=%fused_computation.14 | convolution fusion | flops 2693791744 | bytes 13631488 | tf_op jit(solution)/shard_map/erd,erf->edf/dot_general | solution.py:196
  280.9 8.9 %pad_maximum_fusion = bf16[4,16,96,1024]{3,2,1,0:T(8,128)(2,1)S(1)} fusion(bf16[4,16,32,1024]{3,2,1,0:T(8,128)(2,1)S(1)} %bitcast.339, bf16[4,16,64,1024]{3,2,1,0:T(8,128)(2,1)} %bitcast.346), kind=kLoop, calls=%fused_computation.1 | loop fusion | flops 25165824 | bytes 25165824 | tf_op jit(solution)/shard_map/concatenate | solution.py:198
  289.8 5.5 %copy.143 = bf16[4,16,96,1024]{3,2,0,1:T(8,128)(2,1)} copy(bf16[4,16,96,1024]{3,2,1,0:T(8,128)(2,1)S(1)} %pad_maximum_fusion) | data formatting | bytes 25165824 | tf_op jit(solution)/shard_map/concatenate | solution.py:198
  302.9 7.2 %convolution_convert_fusion.2 = bf16[4,320,1024]{2,1,0:T(8,128)(2,1)S(1)} fusion(bf16[4,1024,1024]{2,1,0:T(8,128)(2,1)} %bitcast.347, bf16[4,320,512]{2,1,0:T(8,128)(2,1)} %copy-done.92, bf16[4,320,512]{2,1,0:T(8,128)(2,1)} %copy-done.91), kind=kOutput, calls=%fused_computation.58 | convolution fusion | flops 2690908160 | bytes 13631488 | tf_op jit(solution)/shard_map/erf,edf->erd/dot_general | solution.py:190
  312.7 4.6 all-to-all-start.9
  320.8 26.5 %all-to-all-done.9 = bf16[8,128,1152]{2,1,0:T(8,128)(2,1)} async-done(((bf16[8,128,1152]{2,1,0:T(8,128)(2,1)}), bf16[8,128,1152]{2,1,0:T(8,128)(2,1)}, u32[]{:S(2)}, u32[]{:S(2)}) %all-to-all-start.9) | async-done | bytes 2359328 | tf_op jit(solution)/shard_map/all_to_all | solution.py:22
  360.9 5.9 %all-to-all-done.10 = bf16[4,128,512]{2,1,0:T(8,128)(2,1)S(1)} async-done(((bf16[4,128,512]{2,1,0:T(8,128)(2,1)}), bf16[4,128,512]{2,1,0:T(8,128)(2,1)S(1)}, u32[]{:S(2)}, u32[]{:S(2)}) %all-to-all-start.10) | async-done | bytes 524320 | tf_op jit(solution)/shard_map/all_to_all | solution.py:22
  366.9 11.6 %fusion.1 = (f32[2,2,512]{2,1,0:T(2,128)S(1)}, f32[2,1536,512,2]{2,1,3,0:T(8,128)}) fusion(f32[2,2,512,1536]{2,3,1,0:T(8,128)} %copy-done, f32[2,2,512]{2,1,0:T(2,128)} %log_add_fusion, bf16[1536,2,64,1]{0,2,3,1:T(8,128)(2,1)S(1)} %bitcast.379, bf16[512,2,2,64]{0,3,2,1:T(8,128)(2,1)S(1)} %bitcast.367), kind=kOutput, calls=%fused_computation.4 | convolution fusion | flops 412088320 | bytes 25837568 | tf_op jit(solution)/shard_map/qkgd,mkd->kgqm/dot_general | solution.py:231
  380.2 7.1 %fusion.3 = bf16[2,2,512,1536]{2,3,1,0:T(8,128)(2,1)S(1)} fusion(f32[2,1536,512,2]{2,1,3,0:T(8,128)} %get-tuple-element.99, f32[2,2,512,1536]{2,3,1,0:T(8,128)S(1)} %bitcast.331, f32[2,2,512]{2,1,0:T(2,128)S(1)} %get-tuple-element.98, f32[2,2,512]{2,1,0:T(2,128)S(1)} %copy-done.55), kind=kLoop, calls=%fused_computation.6 | loop fusion | flops 12582912 | bytes 31473664 | tf_op jit(solution)/shard_map/convert_element_type | solution.py:233
  398.4 6.6 %fusion.6 = f32[2,64,1536,1]{2,1,3,0:T(8,128)S(1)} fusion(bf16[512,2,2,64]{0,3,2,1:T(8,128)(2,1)S(1)} %bitcast.368, f32[2,2,512,1536]{2,3,1,0:T(8,128)} %copy-done, f32[2,2,512]{2,1,0:T(2,128)S(1)} %copy-done.55), kind=kOutput, calls=%fused_computation.15 | convolution fusion | flops 408944640 | bytes 13639680 | tf_op jit(solution)/shard_map/kgqm,qkgd->mkd/dot_general | solution.py:236
  406.9 4.5 collective-permute-start.2
  426.7 18.3 %all-to-all-done.7 = bf16[8,128,1024]{2,1,0:T(8,128)(2,1)S(1)} async-done(((bf16[8,128,1024]{2,1,0:T(8,128)(2,1)}), bf16[8,128,1024]{2,1,0:T(8,128)(2,1)S(1)}, u32[]{:S(2)}, u32[]{:S(2)}) %all-to-all-start.7) | async-done | bytes 2097184 | tf_op jit(solution)/shard_map/all_to_all | solution.py:22
  459.2 5.2 all-to-all-done.12
  464.4 7.5 %all-to-all-start.13 = ((bf16[128,8,832]{2,1,0:T(8,128)(2,1)}), bf16[128,8,832]{2,1,0:T(8,128)(2,1)}, u32[]{:S(2)}, u32[]{:S(2)}) async-start(bf16[128,8,832]{2,1,0:T(8,128)(2,1)} %pad_maximum_fusion.4), calls=%async_computation.13 | async-start | bytes 3670016 | tf_op jit(solution)/shard_map/all_to_all | solution.py:22
  474.3 24.9 %all-to-all-done.13 = bf16[128,8,832]{2,1,0:T(8,128)(2,1)} async-done(((bf16[128,8,832]{2,1,0:T(8,128)(2,1)}), bf16[128,8,832]{2,1,0:T(8,128)(2,1)}, u32[]{:S(2)}, u32[]{:S(2)}) %all-to-all-start.13) | async-done | bytes 1703968 | tf_op jit(solution)/shard_map/all_to_all | solution.py:22
  506.6 7.8 %all-to-all-done.14 = bf16[8,8,3136]{2,1,0:T(8,128)(2,1)S(1)} async-done(((bf16[8,8,3136]{2,1,0:T(8,128)(2,1)}), bf16[8,8,3136]{2,1,0:T(8,128)(2,1)S(1)}, u32[]{:S(2)}, u32[]{:S(2)}) %all-to-all-start.14) | async-done | bytes 401440 | tf_op jit(solution)/shard_map/all_to_all | solution.py:22
  (415 shorter events, 164.3 us)
Async XLA Ops:
  7.2 231.3 %all-gather.3.cloned.1.call-start = ((), (), s32[]{:S(2)}) async-start(), calls=%async_computation.17 | async-start | bytes 13369344 | tf_op jit(solution)/shard_map/all_gather | solution.py:85
  11.8 24.8 %all-to-all-start = ((bf16[4,128,1024]{2,1,0:T(8,128)(2,1)}), bf16[4,128,1024]{2,1,0:T(8,128)(2,1)S(1)}, u32[]{:S(2)}, u32[]{:S(2)}) async-start(bf16[4,128,1024]{2,1,0:T(8,128)(2,1)} %broadcast_in_dim.94), calls=%async_computation | async-start | bytes 2097152 | tf_op jit(solution)/shard_map/all_to_all | solution.py:22
  25.1 59.3 %copy-start.39 = (f32[512,32]{0,1:T(8,128)}, f32[512,32]{0,1:T(8,128)S(1)}, u32[]{:S(2)}) copy-start(f32[512,32]{0,1:T(8,128)S(1)} %slice.348) | copy-start | bytes 196612
  37.9 24.6 %all-to-all-start.1 = ((bf16[16,64,640]{2,1,0:T(8,128)(2,1)}), bf16[16,64,640]{2,1,0:T(8,128)(2,1)S(1)}, u32[]{:S(2)}, u32[]{:S(2)}) async-start(bf16[16,64,640]{2,1,0:T(8,128)(2,1)} %bitcast.360), calls=%async_computation.1 | async-start | bytes 2621440 | tf_op jit(solution)/shard_map/all_to_all | solution.py:22
  63.4 254.0 %copy-start.60 = (f32[1024]{0:T(1024)}, f32[1024]{0:T(1024)S(1)}, u32[]{:S(2)}) copy-start(f32[1024]{0:T(1024)S(1)} %get-tuple-element.48) | copy-start | bytes 12292
  63.4 287.3 %copy-start.62 = (f32[1024]{0:T(1024)}, f32[1024]{0:T(1024)S(1)}, u32[]{:S(2)}) copy-start(f32[1024]{0:T(1024)S(1)} %get-tuple-element.47) | copy-start | bytes 12292
  64.6 20.0 %collective-permute-start.1 = (bf16[512,256]{0,1:T(8,128)(2,1)S(1)}, bf16[512,256]{0,1:T(8,128)(2,1)}, u32[]{:S(2)}, u32[]{:S(2)}) collective-permute-start(bf16[512,256]{0,1:T(8,128)(2,1)S(1)} %slice.477), channel_id=1, source_target_pairs={{32,0},{64,32},{96,64},{33,1},{65,33},{97,65},{34,2},{66,34},{98,6... | collective-permute-start | bytes 786440 | tf_op jit(solution)/shard_map/ppermute | solution.py:33
  65.9 18.7 %collective-permute-start = (bf16[512,256]{0,1:T(8,128)(2,1)S(1)}, bf16[512,256]{0,1:T(8,128)(2,1)}, u32[]{:S(2)}, u32[]{:S(2)}) collective-permute-start(bf16[512,256]{0,1:T(8,128)(2,1)S(1)} %slice.477), channel_id=1, source_target_pairs={{0,32},{32,64},{64,96},{1,33},{33,65},{65,97},{2,34},{34,66},{66,9... | collective-permute-start | bytes 786440 | tf_op jit(solution)/shard_map/ppermute | solution.py:33
  72.2 12.0 %all-to-all-start.2 = ((f32[16,8,128]{2,1,0:T(8,128)}), f32[16,8,128]{2,1,0:T(8,128)S(1)}, u32[]{:S(2)}, u32[]{:S(2)}) async-start(f32[16,8,128]{2,1,0:T(8,128)} %broadcast_in_dim.101), calls=%async_computation.2 | async-start | bytes 131072 | tf_op jit(solution)/shard_map/all_to_all | solution.py:22
  124.8 37.2 %copy-start.15 = (bf16[1,128,1024]{2,1,0:T(8,128)(2,1)S(1)}, bf16[1,128,1024]{2,1,0:T(8,128)(2,1)}, u32[]{:S(2)}) copy-start(bf16[1,128,1024]{2,1,0:T(8,128)(2,1)} %param.18) | copy-start | bytes 786436
  124.8 32.3 %all-to-all-start.4 = ((bf16[16,64,1024]{2,1,0:T(8,128)(2,1)}), bf16[16,64,1024]{2,1,0:T(8,128)(2,1)S(1)}, u32[]{:S(2)}, u32[]{:S(2)}) async-start(bf16[16,64,1024]{2,1,0:T(8,128)(2,1)} %broadcast_in_dim.106), calls=%async_computation.4 | async-start | bytes 4194304 | tf_op jit(solution)/shard_map/all_to_all | solution.py:22
  157.7 9.9 %all-to-all-start.5 = ((s32[8,9,128]{2,1,0:T(8,128)}), s32[8,9,128]{2,1,0:T(8,128)S(1)}, u32[]{:S(2)}, u32[]{:S(2)}) async-start(s32[8,9,128]{2,1,0:T(8,128)} %broadcast_in_dim.107), calls=%async_computation.5 | async-start | bytes 131072 | tf_op jit(solution)/shard_map/all_to_all | solution.py:22
  162.5 188.2 %copy-start.71 = (f32[128]{0:T(128)}, f32[128]{0:T(128)S(1)}, u32[]{:S(2)}) copy-start(f32[128]{0:T(128)S(1)} %add_rsqrt_fusion.2) | copy-start | bytes 1540
  163.4 35.2 %copy-start.25 = (bf16[128,1024]{1,0:T(8,128)(2,1)}, bf16[128,1024]{1,0:T(8,128)(2,1)S(1)}, u32[]{:S(2)}) copy-start(bf16[128,1024]{1,0:T(8,128)(2,1)S(1)} %multiply_convert_fusion.8) | copy-start | bytes 786436
  200.3 31.6 %all-to-all-start.8 = ((bf16[8,128,1024]{2,1,0:T(8,128)(2,1)}), bf16[8,128,1024]{2,1,0:T(8,128)(2,1)}, u32[]{:S(2)}, u32[]{:S(2)}) async-start(bf16[8,128,1024]{2,1,0:T(8,128)(2,1)} %broadcast_in_dim.113), calls=%async_computation.8 | async-start | bytes 4194304 | tf_op jit(solution)/shard_map/all_to_all | solution.py:22
  204.7 313.2 %reduce-scatter.2.cloned.1.call-start = ((), (), s32[]{:S(2)}) async-start(), calls=%async_computation.16 | async-start | bytes 13369344 | tf_op jit(solution)/shard_map/reduce_scatter | solution.py:201
  312.7 34.6 %all-to-all-start.9 = ((bf16[8,128,1152]{2,1,0:T(8,128)(2,1)}), bf16[8,128,1152]{2,1,0:T(8,128)(2,1)}, u32[]{:S(2)}, u32[]{:S(2)}) async-start(bf16[8,128,1152]{2,1,0:T(8,128)(2,1)} %pad_maximum_fusion.2), calls=%async_computation.9 | async-start | bytes 4718592 | tf_op jit(solution)/shard_map/all_to_all | solution.py:22
  319.3 32.3 %copy-start.23 = (bf16[1,128,1024]{2,1,0:T(8,128)(2,1)S(1)}, bf16[1,128,1024]{2,1,0:T(8,128)(2,1)}, u32[]{:S(2)}) copy-start(bf16[1,128,1024]{2,1,0:T(8,128)(2,1)} %param.19) | copy-start | bytes 786436
  353.5 13.2 %all-to-all-start.10 = ((bf16[4,128,512]{2,1,0:T(8,128)(2,1)}), bf16[4,128,512]{2,1,0:T(8,128)(2,1)S(1)}, u32[]{:S(2)}, u32[]{:S(2)}) async-start(bf16[4,128,512]{2,1,0:T(8,128)(2,1)} %pad_maximum_fusion.9), calls=%async_computation.10 | async-start | bytes 1048576 | tf_op jit(solution)/shard_map/all_to_all | solution.py:22
  394.7 18.9 %all-to-all-start.11 = ((f32[16,8,128]{2,1,0:T(8,128)}), f32[16,8,128]{2,1,0:T(8,128)S(1)}, u32[]{:S(2)}, u32[]{:S(2)}) async-start(f32[16,8,128]{2,1,0:T(8,128)} %bitcast.83), calls=%async_computation.11 | async-start | bytes 131072 | tf_op jit(solution)/shard_map/all_to_all | solution.py:22
  406.9 14.2 %collective-permute-start.2 = (bf16[512,256]{0,1:T(8,128)(2,1)}, bf16[512,256]{0,1:T(8,128)(2,1)}, u32[]{:S(2)}, u32[]{:S(2)}) collective-permute-start(bf16[512,256]{0,1:T(8,128)(2,1)} %get-tuple-element.60), channel_id=1, source_target_pairs={{0,32},{32,64},{64,96},{1,33},{33,65},{65,97},{2,34},{34,66},{66,9... | collective-permute-start | bytes 786440 | tf_op jit(solution)/shard_map/ppermute | solution.py:310
  411.4 9.7 %collective-permute-start.3 = (bf16[512,256]{0,1:T(8,128)(2,1)}, bf16[512,256]{0,1:T(8,128)(2,1)}, u32[]{:S(2)}, u32[]{:S(2)}) collective-permute-start(bf16[512,256]{0,1:T(8,128)(2,1)} %get-tuple-element.61), channel_id=1, source_target_pairs={{32,0},{64,32},{96,64},{33,1},{65,33},{97,65},{34,2},{66,34},{98,6... | collective-permute-start | bytes 786440 | tf_op jit(solution)/shard_map/ppermute | solution.py:310
  414.2 30.7 %all-to-all-start.7 = ((bf16[8,128,1024]{2,1,0:T(8,128)(2,1)}), bf16[8,128,1024]{2,1,0:T(8,128)(2,1)S(1)}, u32[]{:S(2)}, u32[]{:S(2)}) async-start(bf16[8,128,1024]{2,1,0:T(8,128)(2,1)} %bitcast_convert_fusion.1), calls=%async_computation.7 | async-start | bytes 4194304 | tf_op jit(solution)/shard_map/all_to_all | solution.py:22
  444.9 19.5 %all-to-all-start.12 = ((bf16[4,128,1024]{2,1,0:T(8,128)(2,1)}), bf16[4,128,1024]{2,1,0:T(8,128)(2,1)}, u32[]{:S(2)}, u32[]{:S(2)}) async-start(bf16[4,128,1024]{2,1,0:T(8,128)(2,1)} %bitcast.385), calls=%async_computation.12 | async-start | bytes 2097152 | tf_op jit(solution)/shard_map/all_to_all | solution.py:22
  464.4 34.7 %all-to-all-start.13 = ((bf16[128,8,832]{2,1,0:T(8,128)(2,1)}), bf16[128,8,832]{2,1,0:T(8,128)(2,1)}, u32[]{:S(2)}, u32[]{:S(2)}) async-start(bf16[128,8,832]{2,1,0:T(8,128)(2,1)} %pad_maximum_fusion.4), calls=%async_computation.13 | async-start | bytes 3670016 | tf_op jit(solution)/shard_map/all_to_all | solution.py:22
  472.4 33.0 %copy-start.11 = (f32[128,1024]{1,0:T(8,128)S(1)}, f32[128,1024]{1,0:T(8,128)}, u32[]{:S(2)}) copy-start(f32[128,1024]{1,0:T(8,128)} %copy-done.9) | copy-start | bytes 1572868
  472.5 33.0 %copy-start.24 = (bf16[1,128,1024]{2,1,0:T(8,128)(2,1)S(1)}, bf16[1,128,1024]{2,1,0:T(8,128)(2,1)}, u32[]{:S(2)}) copy-start(bf16[1,128,1024]{2,1,0:T(8,128)(2,1)} %param.19) | copy-start | bytes 786436
  472.5 33.0 %copy-start.30 = (f32[128,1024]{1,0:T(8,128)S(1)}, f32[128,1024]{1,0:T(8,128)}, u32[]{:S(2)}) copy-start(f32[128,1024]{1,0:T(8,128)} %copy-done.29) | copy-start | bytes 1572868
  472.5 33.0 %copy-start.63 = (f32[1024]{0:T(1024)S(1)}, f32[1024]{0:T(1024)}, u32[]{:S(2)}) copy-start(f32[1024]{0:T(1024)} %copy-done.62) | copy-start | bytes 12292
  472.5 33.0 %copy-start.72 = (f32[128]{0:T(128)S(1)}, f32[128]{0:T(128)}, u32[]{:S(2)}) copy-start(f32[128]{0:T(128)} %copy-done.71) | copy-start | bytes 1540
  472.5 33.0 %copy-start.79 = (f32[128]{0:T(128)S(1)}, f32[128]{0:T(128)}, u32[]{:S(2)}) copy-start(f32[128]{0:T(128)} %copy-done.78) | copy-start | bytes 1540
  501.8 12.6 %all-to-all-start.14 = ((bf16[8,8,3136]{2,1,0:T(8,128)(2,1)}), bf16[8,8,3136]{2,1,0:T(8,128)(2,1)S(1)}, u32[]{:S(2)}, u32[]{:S(2)}) async-start(bf16[8,8,3136]{2,1,0:T(8,128)(2,1)} %broadcast_in_dim.224), calls=%async_computation.14 | async-start | bytes 819200 | tf_op jit(solution)/shard_map/all_to_all | solution.py:22
  (86 other events, 874.2 us)
Sparse Core Ops, SparseCore 0:
  10.8 112.0 all-gather.2
  295.4 91.4 reduce-scatter.1
